TPU v7x, 32 devices: a whole 2x2x4 slice. The times are simulated.
32 devices in a mesh: groups: 2 (over y), seq: 4 (over x, core), dp: 4 (over z).
Axes of the slice: x: 2, y: 2, z: 4, core: 2. Of those that a mesh axis runs over, the one named last changes fastest.
Arguments:
- hidden_states: bfloat16 [8, 8, 256, 1152], P(('groups', 'dp'), 'seq'), parts along dimension 0, may hold values from -80 to 80
- modulation: float32 [8, 3, 1152], P(('groups', 'dp')), parts along dimension 0, may hold values from -0.5 to 1
- qkv_weight: bfloat16 [1152, 1728], P('dp'), may hold values from -0.1875 to 0.1875
- qk_gain: float32 [2, 72], replicated, may hold values from 0.5 to 4
- out_weight: bfloat16 [576, 1152], replicated, may hold values from -0.25 to 0.25
- out_cotangent: bfloat16 [8, 8, 256, 1152], P(('groups', 'dp'), 'seq'), parts along dimension 0, may hold values from -6 to 6
Outputs:
- grad_hidden: bfloat16 [8, 8, 256, 1152], P(('groups', 'dp'), 'seq'), parts along dimension 0
- grad_out_weight: float32 [1152, 1152], P(('groups', 'seq'), 'dp'), parts along dimension 0
There are 2 independent parts, one for each index of `groups`. A program takes and returns all parts, laid end to end along the dimension named above; an argument that names none is the same for every part. Nothing has to cross between parts.
All inputs are finite; a program needn't handle non-finite values.
Results may differ from a plain program's by a relative error of at most 0.012.
The roundings to bfloat16 on the way count: a program that leaves them out, or rounds other values in their place, can miss the bound.
Values may be sent and summed in bfloat16 or wider, within the bound.
A program may use at most 64 MiB of HBM per device.

v0:
```python
import jax
import jax.numpy as jnp
from jax import lax
from jax.sharding import PartitionSpec as P

HEADS = 8
HD = 72


norm_eps = 1e-06


def layer_normed(values):
    centered = values - jnp.mean(values, -1, keepdims=True)
    inverse = lax.rsqrt(jnp.mean(centered * centered, -1, keepdims=True) + norm_eps)
    return (centered * inverse, inverse)


def rms_normed(values, gain_row):
    inverse = lax.rsqrt(jnp.mean(values * values, -1, keepdims=True) + norm_eps)
    return (values * inverse * gain_row, inverse)


def rms_back(values, inverse, gain_row, grad_out):
    scaled = grad_out * gain_row
    return inverse * scaled - values * inverse * inverse * inverse * jnp.mean(
        values * scaled, -1, keepdims=True
    )


def temporal_forward(packed, qk_gain):
    frames, tokens = (packed.shape[0], packed.shape[1])
    score_scale = HD ** (-0.5)
    unpacked = packed.reshape(frames, tokens, 3, HEADS, HD)
    queries = unpacked[:, :, 0].astype(jnp.float32)
    keys_raw = unpacked[:, :, 1].astype(jnp.float32)
    values = unpacked[:, :, 2]
    query_n, query_inv = rms_normed(queries, qk_gain[0])
    key_n, key_inv = rms_normed(keys_raw, qk_gain[1])
    query_b = query_n.astype(jnp.bfloat16)
    key_b = key_n.astype(jnp.bfloat16)
    scores = (
        jnp.einsum("fshd,gshd->shfg", query_b, key_b, preferred_element_type=jnp.float32)
        * score_scale
    )
    shifted = jnp.exp(scores - jnp.max(scores, -1, keepdims=True))
    softmax_probs = shifted / jnp.sum(shifted, -1, keepdims=True)
    probs_b = softmax_probs.astype(jnp.bfloat16)
    attended = jnp.einsum(
        "shfg,gshd->fshd", probs_b, values, preferred_element_type=jnp.float32
    ).astype(jnp.bfloat16)
    stored = (queries, keys_raw, values, query_inv, key_inv, query_b, key_b, softmax_probs, probs_b)
    return (attended.reshape(frames, tokens, HEADS * HD), stored)


def temporal_backward(stored, qk_gain, grad_att):
    queries, keys_raw, values, query_inv, key_inv, query_b, key_b, softmax_probs, probs_b = stored
    frames, tokens = (queries.shape[0], queries.shape[1])
    score_scale = HD ** (-0.5)
    grad_heads = grad_att.reshape(frames, tokens, HEADS, HD)
    grad_values = jnp.einsum(
        "shfg,fshd->gshd", probs_b, grad_heads, preferred_element_type=jnp.float32
    )
    grad_probs = jnp.einsum(
        "fshd,gshd->shfg", grad_heads, values, preferred_element_type=jnp.float32
    )
    grad_scores = (
        softmax_probs
        * (grad_probs - jnp.sum(softmax_probs * grad_probs, -1, keepdims=True))
        * score_scale
    )
    grad_qn = jnp.einsum(
        "shfg,gshd->fshd", grad_scores, key_b.astype(jnp.float32), precision=lax.Precision.HIGHEST
    )
    grad_kn = jnp.einsum(
        "shfg,fshd->gshd", grad_scores, query_b.astype(jnp.float32), precision=lax.Precision.HIGHEST
    )
    grad_query = rms_back(queries, query_inv, qk_gain[0], grad_qn)
    grad_keys = rms_back(keys_raw, key_inv, qk_gain[1], grad_kn)
    stacked = jnp.stack([grad_query, grad_keys, grad_values], axis=2).astype(jnp.bfloat16)
    return stacked.reshape(frames, tokens, 3 * HEADS * HD)


def project_rows(rows_in, weights):
    return (
        jnp.dot(rows_in.reshape(-1, rows_in.shape[-1]), weights, preferred_element_type=jnp.float32)
        .astype(jnp.bfloat16)
        .reshape(rows_in.shape[0], rows_in.shape[1], -1)
    )


def project_back(grad_rows_in, weights):
    flat = grad_rows_in.reshape(-1, grad_rows_in.shape[-1])
    result = lax.dot_general(
        flat, weights, (((1,), (1,)), ((), ())), preferred_element_type=jnp.float32
    )
    return result.astype(jnp.bfloat16).reshape(grad_rows_in.shape[0], grad_rows_in.shape[1], -1)


def shards(hidden_states, modulation, qkv_weight, qk_gain, out_weight, out_cotangent):
    states = hidden_states[0]
    modulation_row = modulation[0]
    cotangent = out_cotangent[0]
    features = states.shape[-1]
    normed, inverse = layer_normed(states.astype(jnp.float32))
    modulated = (normed * (1.0 + modulation_row[1]) + modulation_row[0]).astype(jnp.bfloat16)
    weights = lax.all_gather(qkv_weight, "dp", axis=0, tiled=True)
    packed_frames = project_rows(modulated, weights)
    packed, cotangent_tok = (
        lax.all_to_all(packed_frames, "seq", split_axis=1, concat_axis=0, tiled=True),
        lax.all_to_all(cotangent, "seq", split_axis=1, concat_axis=0, tiled=True),
    )
    attended, stored = temporal_forward(packed, qk_gain)
    gated = (modulation_row[2] * cotangent_tok.astype(jnp.float32)).astype(jnp.bfloat16)
    flat_att = attended.reshape(-1, attended.shape[-1])
    flat_gated = gated.reshape(-1, features)
    seq_share = lax.psum_scatter(
        lax.dot_general(
            flat_att, flat_gated, (((0,), (0,)), ((), ())), preferred_element_type=jnp.float32
        ),
        "seq",
        scatter_dimension=0,
        tiled=True,
    )
    grad_weight = lax.psum_scatter(seq_share, "dp", scatter_dimension=1, tiled=True)
    grad_att = lax.dot_general(
        flat_gated, out_weight, (((1,), (1,)), ((), ())), preferred_element_type=jnp.float32
    ).astype(jnp.bfloat16)
    grad_packed = temporal_backward(stored, qk_gain, grad_att.reshape(attended.shape))
    grad_packed_frames = lax.all_to_all(grad_packed, "seq", split_axis=0, concat_axis=1, tiled=True)
    grad_mod = project_back(grad_packed_frames, weights)
    grad_normed = grad_mod.astype(jnp.float32) * (1.0 + modulation_row[1])
    grad_ln = inverse * (
        grad_normed
        - jnp.mean(grad_normed, -1, keepdims=True)
        - normed * jnp.mean(grad_normed * normed, -1, keepdims=True)
    )
    grad_states = (cotangent.astype(jnp.float32) + grad_ln).astype(jnp.bfloat16)
    return (grad_states[None], grad_weight)


def solution(mesh):
    placed = (
        P(("groups", "dp"), "seq", None, None),
        P(("groups", "dp"), None, None),
        P("dp", None),
        P(),
        P(),
        P(("groups", "dp"), "seq", None, None),
    )
    return jax.shard_map(
        shards,
        mesh=mesh,
        in_specs=placed,
        out_specs=(P(("groups", "dp"), "seq", None, None), P(("groups", "seq"), "dp")),
        check_vma=False,
    )
```

profile of v0, /device:TPU:0, one launch (start us, length us, event | category | flops | bytes accessed | tf_op | source)
XLA Modules:
  0.0 267.0 jit_solution(11605628592592949008)
XLA Ops:
  7.9 3.6 %copy.109 = bf16[1,2,256,1152]{3,1,2,0:T(2,128)(2,1)} copy(bf16[1,2,256,1152]{3,2,1,0:T(8,128)(2,1)} %param.11) | data formatting | bytes 2359296 | tf_op args[5]
  11.5 4.4 %all-to-all-start.1 = ((bf16[2,256,1152]{2,0,1:T(2,128)(2,1)}), bf16[2,256,1152]{2,0,1:T(2,128)(2,1)}, u32[]{:S(2)}, u32[]{:S(2)}) async-start(bf16[2,256,1152]{2,0,1:T(2,128)(2,1)} %bitcast.141), calls=%async_computation.1 | async-start | bytes 2359296 | tf_op jit(solution)/shard_map/all_to_all | solution.py:111
  19.5 72.6 %all-gather.2.cloned.1.call-done = bf16[1152,1728]{1,0:T(8,128)(2,1)} async-done(((bf16[288,1728]{1,0:T(8,128)(2,1)}), bf16[1152,1728]{1,0:T(8,128)(2,1)}) %all-gather.2.cloned.1.call-update) | async-done | bytes 3981328 | tf_op jit(solution)/shard_map/all_gather | solution.py:107
  92.0 6.3 %convolution_convert_fusion.1 = bf16[512,1728]{0,1:T(8,128)(2,1)} fusion(bf16[512,1152]{1,0:T(8,128)(2,1)} %add_convert_fusion.1, bf16[1152,1728]{1,0:T(8,128)(2,1)} %all-gather.2.cloned.1.call-done), kind=kOutput, calls=%fused_computation.10 | convolution fusion | flops 2039316480 | bytes 6930432 | tf_op jit(solution)/shard_map/dot_general | solution.py:86
  98.3 4.8 %reshape.145 = bf16[2,256,1728]{1,0,2:T(2,128)(2,1)} reshape(bf16[512,1728]{0,1:T(8,128)(2,1)} %convolution_convert_fusion.1) | data formatting | bytes 3538944 | tf_op jit(solution)/shard_map/reshape | solution.py:88
  103.1 7.3 %copy.40 = bf16[2,256,1728]{2,0,1:T(2,128)(2,1)} copy(bf16[2,256,1728]{1,0,2:T(2,128)(2,1)} %reshape.145) | data formatting | bytes 3538944 | tf_op jit(solution)/shard_map/reshape | solution.py:88
  110.4 4.5 %all-to-all-start = ((bf16[2,256,1728]{2,0,1:T(2,128)(2,1)}), bf16[2,256,1728]{2,0,1:T(2,128)(2,1)}, u32[]{:S(2)}, u32[]{:S(2)}) async-start(bf16[2,256,1728]{2,0,1:T(2,128)(2,1)} %copy.40), calls=%async_computation | async-start | bytes 3670016 | tf_op jit(solution)/shard_map/all_to_all | solution.py:110
  118.7 1.5 copy.47
  120.3 17.6 %all-to-all-done = bf16[2,256,1728]{2,0,1:T(2,128)(2,1)} async-done(((bf16[2,256,1728]{2,0,1:T(2,128)(2,1)}), bf16[2,256,1728]{2,0,1:T(2,128)(2,1)}, u32[]{:S(2)}, u32[]{:S(2)}) %all-to-all-start) | async-done | bytes 1769504 | tf_op jit(solution)/shard_map/all_to_all | solution.py:110
  137.9 1.7 copy.41
  141.0 6.4 %reshape.146 = bf16[8,64,3,8,72]{4,3,2,1,0:T(8,128)(2,1)} reshape(bf16[4,2,64,1728]{3,2,1,0:T(8,128)(2,1)} %copy.42) | data formatting | bytes 3538944 | tf_op jit(solution)/shard_map/reshape | solution.py:34
  147.4 3.2 %fusion.47 = (bf16[8,64,1,8,72]{4,3,2,1,0:T(8,128)(2,1)}, bf16[8,64,1,8,72]{4,3,2,1,0:T(8,128)(2,1)S(1)}, bf16[8,64,1,8,72]{4,3,2,1,0:T(8,128)(2,1)S(1)}) fusion(bf16[8,64,3,8,72]{4,3,2,1,0:T(8,128)(2,1)} %reshape.146), kind=kLoop, calls=%fused_computation.89 | loop fusion | bytes 3538944 | tf_op jit(solution)/shard_map/slice | solution.py:37
  153.6 5.3 %fusion.48 = (f32[64,8,8]{2,1,0:T(8,128)}, f32[64,8,8,8]{2,3,1,0:T(8,128)}) fusion(f32[72]{0:T(128)} %get-tuple-element.15, f32[8,64,8]{0,2,1:T(8,128)} %add_rsqrt_fusion, bf16[8,64,1,8,72]{4,3,2,1,0:T(8,128)(2,1)S(1)} %get-tuple-element.8, f32[72]{0:T(128)} %get-tuple-element.14, f32[8,64,8]{0,2,1:T(8,128)} %add_rsqrt_fusion.1, ...), kind=kOutput, calls=%fused_computation.90 | convolution fusion | flops 7176199 | bytes 1360448 | tf_op jit(solution)/shard_map/sub | solution.py:46
  158.9 2.9 %fusion.27 = bf16[8,64,8,72]{3,0,2,1:T(8,128)(2,1)S(1)} fusion(bf16[8,64,1,8,72]{4,3,2,1,0:T(8,128)(2,1)} %get-tuple-element.7, f32[64,8,8,8]{2,3,1,0:T(8,128)} %get-tuple-element.17, f32[64,8,8]{2,1,0:T(8,128)} %get-tuple-element.16), kind=kOutput, calls=%fused_computation.54 | convolution fusion | flops 5079040 | bytes 1327104 | tf_op jit(solution)/shard_map/shfg,gshd->fshd/dot_general | solution.py:49
  162.9 2.7 %reshape_reshape.7 = bf16[512,576]{1,0:T(8,128)(2,1)} reshape(bf16[8,64,8,72]{3,2,1,0:T(8,128)(2,1)} %copy.56) | data formatting | bytes 1179648 | tf_op jit(solution)/shard_map/reshape;reshape | solution.py:115
  165.6 4.0 %fusion.57 = f32[576,1152]{1,0:T(8,128)} fusion(bf16[512,576]{1,0:T(8,128)(2,1)} %reshape_reshape.7, bf16[512,1152]{1,0:T(8,128)(2,1)} %bitcast.142), kind=kOutput, calls=%fused_computation.91 | convolution fusion | flops 679477248 | bytes 4423680 | tf_op jit(solution)/shard_map/dot_general | solution.py:118
  169.7 1.8 fusion.7
  171.5 1.8 convolution_convert_fusion.4
  173.3 1.7 reshape.157
  175.0 2.6 copy.50
  177.6 3.7 %multiply_reduce_fusion.2 = (f32[64,8,8]{2,1,0:T(8,128)S(1)}, f32[64,8,8,8]{2,3,1,0:T(8,128)S(1)}) fusion(f32[64,8,8,8]{2,3,1,0:T(8,128)} %get-tuple-element.17, f32[64,8,8]{2,1,0:T(8,128)} %get-tuple-element.16, bf16[8,64,8,72]{3,0,2,1:T(8,128)(2,1)} %copy.50, bf16[8,64,1,8,72]{4,3,2,1,0:T(8,128)(2,1)} %get-tuple-element.7), kind=kOutput, calls=%fused_computation.46 | convolution fusion | flops 4812800 | bytes 1474560 | tf_op jit(solution)/shard_map/fshd,gshd->shfg/dot_general | solution.py:64
  181.4 3.6 %fusion.24 = (f32[8,64,8]{0,2,1:T(8,128)S(1)}, f32[64,8,72,8]{2,3,1,0:T(8,128)S(1)}) fusion(f32[72]{0:T(128)S(1)} %copy-done.19, bf16[8,64,1,8,72]{4,3,2,1,0:T(8,128)(2,1)S(1)} %copy-done.4, f32[64,8,8,8]{2,3,1,0:T(8,128)S(1)} %get-tuple-element.19, f32[64,8,8]{2,1,0:T(8,128)S(1)} %get-tuple-element.18, f32[64,8,8,8]{2,3,1,0:T(8,128)S(1)} %copy-done.22, ...), kind=kOutput, calls=%fused_computation.42 | convolution fusion | flops 30797824 | bytes 2687552 | tf_op jit(solution)/shard_map/shfg,gshd->fshd/dot_general | solution.py:72
  185.1 3.3 %fusion.22 = (f32[8,64,8]{0,2,1:T(8,128)S(1)}, f32[64,8,72,8]{2,3,1,0:T(8,128)S(1)}) fusion(f32[72]{0:T(128)S(1)} %copy-done.20, bf16[8,64,1,8,72]{4,3,2,1,0:T(8,128)(2,1)S(1)} %get-tuple-element.8, f32[64,8,8,8]{2,3,1,0:T(8,128)S(1)} %get-tuple-element.19, f32[64,8,8]{2,1,0:T(8,128)S(1)} %get-tuple-element.18, f32[64,8,8,8]{2,3,1,0:T(8,128)S(1)} %copy-done.22, ...), kind=kOutput, calls=%fused_computation.40 | convolution fusion | flops 30797824 | bytes 2687552 | tf_op jit(solution)/shard_map/shfg,fshd->gshd/dot_general | solution.py:75
  189.1 3.3 %fusion.29 = (bf16[8,64,1,8,72]{4,0,3,1,2:T(8,128)(2,1)S(1)}, bf16[8,64,1,8,72]{4,0,3,1,2:T(8,128)(2,1)S(1)}) fusion(f32[64,8,72,8]{2,3,1,0:T(8,128)S(1)} %get-tuple-element.21, f32[8,64,8]{0,2,1:T(8,128)S(1)} %broadcast_multiply_fusion, f32[72]{0:T(128)S(1)} %copy-done.20, f32[8,64,8]{0,2,1:T(8,128)S(1)} %copy-done.5, ...), kind=kLoop, calls=%fused_computation.58 | loop fusion | flops 5308416 | bytes 4784704 | tf_op jit(solution)/shard_map/stack | solution.py:80
  193.2 2.2 copy.53
  195.4 5.7 %convert_element_type.136 = bf16[8,64,1728]{2,1,0:T(8,128)(2,1)} reshape(bf16[8,64,3,8,72]{4,3,2,1,0:T(8,128)(2,1)} %copy.53) | data formatting | bytes 3538944 | tf_op jit(solution)/shard_map/convert_element_type | solution.py:80
  201.1 26.4 %all_to_all.39 = bf16[8,64,1728]{2,1,0:T(8,128)(2,1)S(1)} all-to-all(bf16[8,64,1728]{2,1,0:T(8,128)(2,1)} %convert_element_type.136), channel_id=1, replica_groups=mesh['groups'=2,'seq'=4,'dp'=4] {'seq'}, dimensions={0} | all-to-all | bytes 3538944 | tf_op jit(solution)/shard_map/all_to_all | solution.py:130
  228.9 2.5 copy.60
  231.5 6.8 %multiply_reduce_fusion.1 = (f32[512]{0:T(512)S(1)}, f32[512]{0:T(512)S(1)}, f32[512,1152]{1,0:T(8,128)}) fusion(f32[1152]{0:T(1024)S(1)} %copy-done.9, f32[512]{0:T(512)S(1)} %bitcast.149, f32[512]{0:T(512)S(1)} %bitcast.147, bf16[1,2,256,1152]{3,2,1,0:T(8,128)(2,1)S(1)} %copy-done.2, bf16[512,1728]{1,0:T(8,128)(2,1)} %bitcast.144, ...), kind=kOutput, calls=%fused_computation.28 | convolution fusion | flops 2043739136 | bytes 9302528 | tf_op jit(solution)/shard_map/dot_general | solution.py:94
  238.3 4.0 %add_convert_fusion = bf16[1,2,256,1152]{3,2,1,0:T(8,128)(2,1)} fusion(f32[1,2,256,1152]{3,2,1,0:T(8,128)} %bitcast.143, bf16[1,2,256,1152]{3,2,1,0:T(8,128)(2,1)} %param.11, bf16[1,2,256,1152]{3,2,1,0:T(8,128)(2,1)S(1)} %copy-done.2, f32[2,256]{1,0:T(2,128)S(1)} %div.50, f32[2,256]{1,0:T(2,128)S(1)} %copy-done.12, f32[2,256]{1,0:T(2,128)S(1)} %div.48, ...), kind=kLoop, calls=%fused_computation.25 | loop fusion | flops 6488064 | bytes 5911040 | tf_op jit(solution)/shard_map/convert_element_type | solution.py:138
  242.4 16.3 %reduce-scatter.7.cloned.1.call-done = f32[288,144]{1,0:T(8,128)} async-done(((f32[1152,144]{1,0:T(8,128)}), f32[288,144]{1,0:T(8,128)}) %reduce-scatter.7.cloned.1.call-update) | async-done | bytes 165904
  258.6 1.8 copy.61
  (84 shorter events, 16.6 us)
Async XLA Ops:
  7.2 164.3 %copy-start = (bf16[576,1152]{1,0:T(8,128)(2,1)S(1)}, bf16[576,1152]{1,0:T(8,128)(2,1)}, u32[]{:S(2)}) copy-start(bf16[576,1152]{1,0:T(8,128)(2,1)} %param.10) | copy-start | bytes 3981316
  7.2 84.8 %all-gather.2.cloned.1.call-start = ((), (), s32[]{:S(2)}) async-start(), calls=%async_computation.5 | async-start | bytes 5160960 | tf_op jit(solution)/shard_map/all_gather | solution.py:107
  7.9 8.0 %copy-start.2 = (bf16[1,2,256,1152]{3,2,1,0:T(8,128)(2,1)S(1)}, bf16[1,2,256,1152]{3,2,1,0:T(8,128)(2,1)}, u32[]{:S(2)}) copy-start(bf16[1,2,256,1152]{3,2,1,0:T(8,128)(2,1)} %param.6) | copy-start | bytes 3538948
  11.5 5.8 %copy-start.13 = (f32[1,3,1152]{2,0,1:T(1,128)S(1)}, f32[1,3,1152]{2,0,1:T(1,128)}, u32[]{:S(2)}) copy-start(f32[1,3,1152]{2,0,1:T(1,128)} %param.7) | copy-start | bytes 41476
  11.5 98.9 %all-to-all-start.1 = ((bf16[2,256,1152]{2,0,1:T(2,128)(2,1)}), bf16[2,256,1152]{2,0,1:T(2,128)(2,1)}, u32[]{:S(2)}, u32[]{:S(2)}) async-start(bf16[2,256,1152]{2,0,1:T(2,128)(2,1)} %bitcast.141), calls=%async_computation.1 | async-start | bytes 2359296 | tf_op jit(solution)/shard_map/all_to_all | solution.py:111
  16.2 1.1 copy-start.11
  16.2 1.1 copy-start.15
  17.3 0.6 copy-start.17
  17.3 0.6 copy-start.8
  17.3 99.8 %copy-start.10 = (f32[1152]{0:T(1024)}, f32[1152]{0:T(1024)S(1)}, u32[]{:S(2)}) copy-start(f32[1152]{0:T(1024)S(1)} %get-tuple-element.5) | copy-start | bytes 13828
  110.4 4.8 %copy-start.21 = (f32[2,72]{1,0:T(2,128)S(1)}, f32[2,72]{1,0:T(2,128)}, u32[]{:S(2)}) copy-start(f32[2,72]{1,0:T(2,128)} %param.9) | copy-start | bytes 1732
  110.4 27.5 %all-to-all-start = ((bf16[2,256,1728]{2,0,1:T(2,128)(2,1)}), bf16[2,256,1728]{2,0,1:T(2,128)(2,1)}, u32[]{:S(2)}, u32[]{:S(2)}) async-start(bf16[2,256,1728]{2,0,1:T(2,128)(2,1)} %copy.40), calls=%async_computation | async-start | bytes 3670016 | tf_op jit(solution)/shard_map/all_to_all | solution.py:110
  114.9 114.0 %reduce-scatter.5.cloned.1.call-start = ((), (), s32[]{:S(2)}) async-start(), calls=%async_computation.6 | async-start | bytes 3317760 | tf_op jit(solution)/shard_map/reduce_scatter | solution.py:117
  150.6 1.5 copy-start.3
  169.6 89.0 %reduce-scatter.7.cloned.1.call-start = ((), (), s32[]{:S(2)}) async-start(), calls=%async_computation.7 | async-start | bytes 1474560
  177.6 3.7 %copy-start.4 = (bf16[8,64,1,8,72]{4,3,2,1,0:T(8,128)(2,1)S(1)}, bf16[8,64,1,8,72]{4,3,2,1,0:T(8,128)(2,1)}, u32[]{:S(2)}) copy-start(bf16[8,64,1,8,72]{4,3,2,1,0:T(8,128)(2,1)} %copy-done.3) | copy-start | bytes 1769476
  177.6 3.7 %copy-start.5 = (f32[8,64,8]{0,2,1:T(8,128)S(1)}, f32[8,64,8]{0,2,1:T(8,128)}, u32[]{:S(2)}) copy-start(f32[8,64,8]{0,2,1:T(8,128)} %add_rsqrt_fusion) | copy-start | bytes 49156
  177.6 3.7 %copy-start.19 = (f32[72]{0:T(128)S(1)}, f32[72]{0:T(128)}, u32[]{:S(2)}) copy-start(f32[72]{0:T(128)} %get-tuple-element.14) | copy-start | bytes 868
  177.6 3.7 %copy-start.20 = (f32[72]{0:T(128)S(1)}, f32[72]{0:T(128)}, u32[]{:S(2)}) copy-start(f32[72]{0:T(128)} %get-tuple-element.15) | copy-start | bytes 868
  177.6 3.7 %copy-start.22 = (f32[64,8,8,8]{2,3,1,0:T(8,128)S(1)}, f32[64,8,8,8]{2,3,1,0:T(8,128)}, u32[]{:S(2)}) copy-start(f32[64,8,8,8]{2,3,1,0:T(8,128)} %get-tuple-element.17) | copy-start | bytes 393220
  177.6 3.7 %copy-start.23 = (f32[64,8,8]{2,1,0:T(8,128)S(1)}, f32[64,8,8]{2,1,0:T(8,128)}, u32[]{:S(2)}) copy-start(f32[64,8,8]{2,1,0:T(8,128)} %get-tuple-element.16) | copy-start | bytes 49156
  181.4 3.7 %copy-start.6 = (f32[8,64,8]{0,2,1:T(8,128)S(1)}, f32[8,64,8]{0,2,1:T(8,128)}, u32[]{:S(2)}) copy-start(f32[8,64,8]{0,2,1:T(8,128)} %add_rsqrt_fusion.1) | copy-start | bytes 49156
  185.1 3.4 %copy-start.7 = (bf16[8,64,8,72]{3,0,2,1:T(8,128)(2,1)S(1)}, bf16[8,64,8,72]{3,0,2,1:T(8,128)(2,1)}, u32[]{:S(2)}) copy-start(bf16[8,64,8,72]{3,0,2,1:T(8,128)(2,1)} %copy.50) | copy-start | bytes 1769476
  228.9 2.5 copy-start.9
  228.9 2.5 copy-start.16
  228.9 2.5 copy-start.18
  231.5 6.8 %copy-start.12 = (f32[2,256]{1,0:T(2,128)S(1)}, f32[2,256]{1,0:T(2,128)}, u32[]{:S(2)}) copy-start(f32[2,256]{1,0:T(2,128)} %copy-done.11) | copy-start | bytes 6148
  231.5 6.8 %copy-start.14 = (f32[2,256]{1,0:T(2,128)S(1)}, f32[2,256]{1,0:T(2,128)}, u32[]{:S(2)}) copy-start(f32[2,256]{1,0:T(2,128)} %get-tuple-element.10) | copy-start | bytes 6148
  238.3 22.1 %copy-start.1 = (bf16[576,1152]{1,0:T(8,128)(2,1)S(1)}, bf16[576,1152]{1,0:T(8,128)(2,1)}, u32[]{:S(2)}) copy-start(bf16[576,1152]{1,0:T(8,128)(2,1)} %param.10) | copy-start | bytes 3981316
Sparse Core Ops, SparseCore 0:
  9.6 82.3 all-gather.1
  169.7 32.4 reduce-scatter.4
  231.6 27.0 reduce-scatter.6
where the time goes:
time: 268 us; the launch traced here: 267 us
  waiting for transfers between devices  107 us (40%)
  local copies, waits for them, and re-layouts  55.4 us (21%)
  matrix products  38.3 us (14%)
  blocking collectives  26.4 us (10%)
  other arithmetic  16.2 us (6%)
  between operations  14.1 us (5%)
  starting transfers between devices  9.23 us (3%)
    all_gather x1, waiting for transfers between devices, shards(): weights = lax.all_gather(qkv_weight, 'dp', axis=0, tiled=True)  72.6 us
    all_to_all x1, blocking collectives, shards(): lax.all_to_all(grad_packed, 'seq', split_axis=0, concat_axis=1, tiled=True)  26.4 us
    all_to_all x1, waiting for transfers between devices, shards(): lax.all_to_all(packed_frames, 'seq', split_axis=1, concat_axis=0, tiled=T...  17.6 us
    unnamed x4, waiting for transfers between devices  17 us
    reshape x2, local copies, waits for them, and re-layouts, project_rows(): return jnp.dot(rows_in.reshape(-1, rows_in.shape[-1]), weights, preferred...  12.1 us
    unnamed x53, local copies, waits for them, and re-layouts  8.54 us
    dot_general x1, matrix products, project_back(): lax.dot_general(flat, weights, (((1,), (1,)), ((), ())), preferred_elemen...  6.78 us
    reshape x1, local copies, waits for them, and re-layouts, temporal_forward(): unpacked = packed.reshape(frames, tokens, 3, HEADS, HD)  6.37 us
  transfers between devices with their start and end apart: 5, of which 3 were waited for; matrix products, arithmetic and copies ran while one was open for 27% of the time, Pallas kernels for 0%

commit v1 on v0

v1 whole, which is shorter than its diff:
```python
import functools

import jax
import jax.numpy as jnp
import numpy as np
from jax import lax
from jax.experimental import pallas as pl
from jax.experimental.pallas import tpu as pltpu
from jax.sharding import PartitionSpec as P

HEADS = 8
HD = 72
WIDE = HEADS * HD
LANES = 128
PAD = -(-WIDE // LANES) * LANES
EPS = 1e-06
MESH = pl.DeviceIdType.MESH
F32 = jnp.float32
BF16 = jnp.bfloat16


def head_tiles(head):
    return range(head * HD // LANES, (head * HD + HD - 1) // LANES + 1)


def dot_nn(a, b):
    return lax.dot_general(a, b, (((1,), (0,)), ((), ())), preferred_element_type=F32)


def dot_nt(a, b):
    return lax.dot_general(a, b, (((1,), (1,)), ((), ())), preferred_element_type=F32)


def dot_tn(a, b):
    return lax.dot_general(a, b, (((0,), (0,)), ((), ())), preferred_element_type=F32)


def head_sum(values, ones):
    high = values.astype(BF16)
    low = (values - high.astype(F32)).astype(BF16)
    return dot_nn(high, ones) + dot_nn(low, ones)


def head_window(array, head, masked):
    tiles = head_tiles(head)
    low = tiles[0] * LANES
    window = array[:, low : low + len(tiles) * LANES]
    if not masked:
        return window
    lane = lax.broadcasted_iota(jnp.int32, window.shape, 1) + low
    inside = (lane >= head * HD) & (lane < head * HD + HD)
    return jnp.where(inside, window, jnp.zeros_like(window))


def add_window(tiles_so_far, head, window):
    for place, tile in enumerate(head_tiles(head)):
        piece = window[:, place * LANES : (place + 1) * LANES]
        tiles_so_far[tile] = piece if tiles_so_far[tile] is None else tiles_so_far[tile] + piece


def kernel(
    sizes,
    hidden,
    cotangent,
    w_in,
    mod,
    gains,
    out_w,
    ones,
    grad_hidden,
    grad_w,
    hid_tok,
    cot_tok,
    gh_tok,
    weights,
    normed_s,
    rinv_s,
    q_s,
    k_s,
    v_s,
    rq_s,
    rk_s,
    qn_s,
    kn_s,
    att_s,
    ga_s,
    probs_s,
    x_send,
    x_recv,
    own_sem,
    w_send,
    w_recv,
    w_own,
):
    nseq, ndp, frames, chunks, tokens, width, gather_here = sizes
    mine = frames // nseq
    rows = frames * tokens
    block = chunks * tokens
    group = lax.axis_index("groups")
    seq = lax.axis_index("seq")
    dp = lax.axis_index("dp")
    core = lax.rem(seq, 2)
    sibling = seq + 1 - 2 * core
    seq_peers = [lax.rem(seq + i, nseq) for i in range(1, nseq)]

    barrier = pltpu.get_barrier_semaphore()
    count = nseq - 1
    for peer in seq_peers:
        pl.semaphore_signal(barrier, inc=1, device_id={"seq": peer}, device_id_type=MESH)
    if gather_here:
        for i in range(1, ndp):
            pl.semaphore_signal(
                barrier, inc=1, device_id={"dp": lax.rem(dp + i, ndp)}, device_id_type=MESH
            )
        pl.semaphore_signal(barrier, inc=1, device_id={"groups": 1 - group}, device_id_type=MESH)
        count += ndp
    pl.semaphore_wait(barrier, count)

    def frames_of(device):
        return pl.ds(device * mine, mine)

    def tokens_of(device, chunk):
        return pl.ds(pl.multiple_of(device * block + chunk * tokens, tokens), tokens)

    def inward(kind, chunk, i):
        source, target = ((hidden, hid_tok), (cotangent, cot_tok))[kind]
        return pltpu.make_async_remote_copy(
            src_ref=source.at[:, tokens_of(seq_peers[i], chunk), :],
            dst_ref=target.at[chunk, frames_of(seq)],
            send_sem=x_send.at[kind, chunk, i],
            recv_sem=x_recv.at[kind, chunk, i],
            device_id={"seq": seq_peers[i]},
            device_id_type=MESH,
        )

    def inward_own(kind, chunk):
        source, target = ((hidden, hid_tok), (cotangent, cot_tok))[kind]
        return pltpu.make_async_copy(
            source.at[:, tokens_of(seq, chunk), :],
            target.at[chunk, frames_of(seq)],
            own_sem.at[kind, chunk],
        )

    def outward(chunk, i):
        return pltpu.make_async_remote_copy(
            src_ref=gh_tok.at[chunk, frames_of(seq_peers[i])],
            dst_ref=grad_hidden.at[:, tokens_of(seq, chunk), :],
            send_sem=x_send.at[2, chunk, i],
            recv_sem=x_recv.at[2, chunk, i],
            device_id={"seq": seq_peers[i]},
            device_id_type=MESH,
        )

    def outward_own(chunk):
        return pltpu.make_async_copy(
            gh_tok.at[chunk, frames_of(seq)],
            grad_hidden.at[:, tokens_of(seq, chunk), :],
            own_sem.at[2, chunk],
        )

    shard = width // ndp
    half = shard // 2

    def piece(source, which):
        return weights.at[pl.ds(pl.multiple_of(source * shard + which * half, 16), half), :]

    def along_dp(i):
        return pltpu.make_async_remote_copy(
            src_ref=w_in.at[pl.ds(pl.multiple_of(group * half, 16), half), :],
            dst_ref=piece(dp, group),
            send_sem=w_send.at[0, i],
            recv_sem=w_recv.at[0, i],
            device_id={"dp": lax.rem(dp + i, ndp)},
            device_id_type=MESH,
        )

    def hand_on(step, i, which, target):
        source = lax.rem(dp + ndp - i, ndp)
        return pltpu.make_async_remote_copy(
            src_ref=piece(source, which),
            dst_ref=piece(source, which),
            send_sem=w_send.at[step, i],
            recv_sem=w_recv.at[step, i],
            device_id=target,
            device_id_type=MESH,
        )

    to_group = {"groups": 1 - group}
    to_core = {"seq": sibling}

    if gather_here:

        @pl.when(lax.rem(dp, 2) == core)
        def _():
            for i in range(1, ndp):
                along_dp(i).start()

        own_weights = pltpu.make_async_copy(
            w_in, weights.at[pl.ds(pl.multiple_of(dp * shard, 16), shard), :], w_own
        )
    else:
        own_weights = pltpu.make_async_copy(w_in, weights, w_own)
    for kind in range(2):
        for chunk in range(chunks):
            for i in range(nseq - 1):
                inward(kind, chunk, i).start()
    own_weights.start()
    for kind in range(2):
        for chunk in range(chunks):
            inward_own(kind, chunk).start()

    if gather_here:

        def relays(i):
            return lax.rem(lax.rem(dp + ndp - i, ndp), 2) == core

        for i in range(1, ndp):

            @pl.when(relays(i))
            def _():
                along_dp(i).wait_recv()
                hand_on(1, i, group, to_group).start()
                hand_on(2, i, group, to_core).start()

        for i in range(1, ndp):

            @pl.when(relays(i))
            def _():
                hand_on(1, i, 1 - group, to_group).wait_recv()
                hand_on(3, i, 1 - group, to_core).start()

        for i in range(1, ndp):

            @pl.when(jnp.logical_not(relays(i)))
            def _():
                hand_on(2, i, group, to_core).wait_recv()
                hand_on(3, i, 1 - group, to_core).wait_recv()

        for i in range(1, ndp):

            @pl.when(relays(i))
            def _():
                hand_on(1, i, group, to_group).wait_send()
                hand_on(2, i, group, to_core).wait_send()
                hand_on(3, i, 1 - group, to_core).wait_send()

        @pl.when(lax.rem(dp, 2) == core)
        def _():
            for i in range(1, ndp):
                along_dp(i).wait_send()

    own_weights.wait()

    scale = HD ** (-0.5)
    k_low = WIDE - (PAD - WIDE)
    v_low = 2 * WIDE

    def forward(chunk, carry):
        for i in range(nseq - 1):
            inward(0, chunk, i).wait()
        inward_own(0, chunk).wait()
        states = hid_tok[chunk].reshape(rows, width).astype(F32)
        centered = states - jnp.mean(states, -1, keepdims=True)
        rinv = lax.rsqrt(jnp.mean(centered * centered, -1, keepdims=True) + EPS)
        normed = centered * rinv
        normed_s[chunk] = normed
        rinv_s[chunk] = rinv
        modulated = (normed * (1.0 + mod[1:2, :]) + mod[0:1, :]).astype(BF16)
        q = dot_nn(modulated, weights[:, 0:PAD]).astype(BF16)
        k = pltpu.roll(dot_nn(modulated, weights[:, k_low : k_low + PAD]), WIDE, 1).astype(BF16)
        v = dot_nn(modulated, weights[:, v_low : v_low + WIDE]).astype(BF16)
        q_s[chunk] = q
        k_s[chunk] = k
        v = jnp.concatenate([v, jnp.zeros((rows, PAD - WIDE), BF16)], axis=1)
        v_s[chunk] = v
        q32 = q.astype(F32)
        k32 = k.astype(F32)
        rq = lax.rsqrt(head_sum(q32 * q32, ones[...]) * (1.0 / HD) + EPS)
        rk = lax.rsqrt(head_sum(k32 * k32, ones[...]) * (1.0 / HD) + EPS)
        rq_s[chunk] = rq
        rk_s[chunk] = rk
        qn = (q32 * rq * gains[0:1, :]).astype(BF16)
        kn = (k32 * rk * gains[1:2, :]).astype(BF16)
        qn_s[chunk] = qn
        kn_s[chunk] = kn
        down = lax.broadcasted_iota(jnp.int32, (rows, rows), 0)
        along = lax.broadcasted_iota(jnp.int32, (rows, rows), 1)
        same = ((down ^ along) & (tokens - 1)) == 0
        attended = [None] * (PAD // LANES)
        for head in range(HEADS):
            scores = dot_nt(head_window(kn, head, True), head_window(qn, head, False)) * scale
            scores = jnp.where(same, scores, -1e30)
            shifted = jnp.exp(scores - jnp.max(scores, 0, keepdims=True))
            probs = shifted * (1.0 / jnp.sum(shifted, 0, keepdims=True))
            probs_s[chunk, head] = probs
            add_window(attended, head, dot_tn(probs.astype(BF16), head_window(v, head, True)))
        att_s[chunk] = jnp.concatenate(attended, axis=1).astype(BF16)
        return carry

    lax.fori_loop(0, chunks, forward, 0)

    def middle(chunk, carry):
        for i in range(nseq - 1):
            inward(1, chunk, i).wait()
        inward_own(1, chunk).wait()
        gated = (mod[2:3, :] * cot_tok[chunk].reshape(rows, width).astype(F32)).astype(BF16)
        ga = dot_nt(gated, out_w[...]).astype(BF16)
        ga_s[chunk] = jnp.concatenate([ga, jnp.zeros((rows, PAD - WIDE), BF16)], axis=1)
        share = dot_tn(att_s[chunk][:, 0:WIDE], gated)

        @pl.when(chunk == 0)
        def _():
            grad_w[...] = share

        @pl.when(chunk > 0)
        def _():
            grad_w[...] += share

        return carry

    lax.fori_loop(0, chunks, middle, 0)

    def backward(chunk, carry):
        qn = qn_s[chunk]
        kn = kn_s[chunk]
        v = v_s[chunk]
        ga = ga_s[chunk]
        grad_qn = [None] * (PAD // LANES)
        grad_kn = [None] * (PAD // LANES)
        grad_v = [None] * (PAD // LANES)
        for head in range(HEADS):
            probs = probs_s[chunk, head]
            ga_head = head_window(ga, head, True)
            grad_probs = dot_nt(head_window(v, head, False), ga_head)
            total = jnp.sum(probs * grad_probs, 0, keepdims=True)
            grad_scores = (probs * (grad_probs - total) * scale).astype(BF16)
            add_window(grad_v, head, dot_nn(probs.astype(BF16), ga_head))
            add_window(grad_qn, head, dot_tn(grad_scores, head_window(kn, head, True)))
            add_window(grad_kn, head, dot_nn(grad_scores, head_window(qn, head, True)))

        def through_norm(raw, inverse, gain, grads):
            raw = raw.astype(F32)
            scaled = jnp.concatenate(grads, axis=1) * gain
            mean = head_sum(raw * scaled, ones[...]) * (1.0 / HD)
            return inverse * scaled - raw * inverse * inverse * inverse * mean

        grad_q = through_norm(q_s[chunk], rq_s[chunk], gains[0:1, :], grad_qn).astype(BF16)
        grad_k = pltpu.roll(
            through_norm(k_s[chunk], rk_s[chunk], gains[1:2, :], grad_kn), PAD - WIDE, 1
        ).astype(BF16)
        grad_v = jnp.concatenate(grad_v, axis=1)[:, 0:WIDE].astype(BF16)
        grad_mod = (
            dot_nt(grad_q, weights[:, 0:PAD])
            + dot_nt(grad_k, weights[:, k_low : k_low + PAD])
            + dot_nt(grad_v, weights[:, v_low : v_low + WIDE])
        ).astype(BF16)
        normed = normed_s[chunk]
        grad_normed = grad_mod.astype(F32) * (1.0 + mod[1:2, :])
        grad_ln = rinv_s[chunk] * (
            grad_normed
            - jnp.mean(grad_normed, -1, keepdims=True)
            - normed * jnp.mean(grad_normed * normed, -1, keepdims=True)
        )
        out = cot_tok[chunk].reshape(rows, width).astype(F32) + grad_ln
        gh_tok[chunk] = out.astype(BF16).reshape(frames, tokens, width)
        for i in range(nseq - 1):
            outward(chunk, i).start()
        outward_own(chunk).start()
        return carry

    lax.fori_loop(0, chunks, backward, 0)
    for chunk in range(chunks):
        for i in range(nseq - 1):
            outward(chunk, i).wait()
        outward_own(chunk).wait()


def shards(nseq, ndp, hidden_states, modulation, qkv_weight, qk_gain, out_weight, out_cotangent):
    mine, all_tokens, width = hidden_states.shape[1:]
    frames = mine * nseq
    block = all_tokens // nseq
    tokens = min(block, max(16, 256 // frames))
    chunks = block // tokens
    rows = frames * tokens
    gather_here = qkv_weight.shape[0] % 32 == 0
    if not gather_here:
        qkv_weight = lax.all_gather(qkv_weight, "dp", axis=0, tiled=True)
    gains = jnp.pad(jnp.tile(qk_gain, (1, HEADS)), ((0, 0), (0, PAD - WIDE)))
    lane = np.arange(PAD)
    inside = (lane < WIDE)[:, None] & (lane[:, None] // HD == lane[None, :] // HD)
    ones = jnp.asarray(inside.astype(np.float32), BF16)
    sizes = (nseq, ndp, frames, chunks, tokens, width, gather_here)
    anywhere = pl.BlockSpec(memory_space=pl.ANY)
    vmem = pl.BlockSpec(memory_space=pltpu.VMEM)

    def wide(dtype):
        return pltpu.VMEM((chunks, rows, PAD), dtype)

    by_token = pltpu.VMEM((chunks, frames, tokens, width), BF16)
    grad_hidden, share = pl.pallas_call(
        functools.partial(kernel, sizes),
        out_shape=(
            jax.ShapeDtypeStruct((mine, all_tokens, width), BF16),
            jax.ShapeDtypeStruct((WIDE, width), F32),
        ),
        in_specs=[anywhere, anywhere, anywhere, vmem, vmem, vmem, vmem],
        out_specs=(anywhere, vmem),
        scratch_shapes=[
            by_token,
            by_token,
            by_token,
            pltpu.VMEM((width, 3 * WIDE), BF16),
            pltpu.VMEM((chunks, rows, width), F32),
            pltpu.VMEM((chunks, rows, 1), F32),
            wide(BF16),
            wide(BF16),
            wide(BF16),
            wide(F32),
            wide(F32),
            wide(BF16),
            wide(BF16),
            wide(BF16),
            wide(BF16),
            pltpu.VMEM((chunks, HEADS, rows, rows), F32),
            pltpu.SemaphoreType.DMA((3, chunks, nseq - 1)),
            pltpu.SemaphoreType.DMA((3, chunks, nseq - 1)),
            pltpu.SemaphoreType.DMA((3, chunks)),
            pltpu.SemaphoreType.DMA((4, ndp)),
            pltpu.SemaphoreType.DMA((4, ndp)),
            pltpu.SemaphoreType.DMA,
        ],
        compiler_params=pltpu.CompilerParams(
            collective_id=0, has_side_effects=True, vmem_limit_bytes=56 * 2**20
        ),
        cost_estimate=pl.CostEstimate(
            flops=12_000_000_000, bytes_accessed=20_000_000, transcendentals=2_000_000
        ),
    )(hidden_states[0], out_cotangent[0], qkv_weight, modulation[0], gains, out_weight, ones)
    share = lax.psum_scatter(share, "seq", scatter_dimension=0, tiled=True)
    share = lax.psum_scatter(share, "dp", scatter_dimension=1, tiled=True)
    return (grad_hidden[None], share)


def solution(mesh):
    placed = (
        P(("groups", "dp"), "seq", None, None),
        P(("groups", "dp"), None, None),
        P("dp", None),
        P(),
        P(),
        P(("groups", "dp"), "seq", None, None),
    )
    return jax.shard_map(
        functools.partial(shards, mesh.shape["seq"], mesh.shape["dp"]),
        mesh=mesh,
        in_specs=placed,
        out_specs=(P(("groups", "dp"), "seq", None, None), P(("groups", "seq"), "dp")),
        check_vma=False,
    )
```

time: 268 us -> 161 us (0.60)
  Pallas kernels: 0 us -> 68.8 us
  local copies, waits for them, and re-layouts: 55.4 us -> 7.96 us
  matrix products: 38.3 us -> 0 us
  waiting for transfers between devices: 107 us -> 70.3 us
  blocking collectives: 26.4 us -> 0 us
  other arithmetic: 16.2 us -> 0 us
  starting transfers between devices: 9.23 us -> 0.08 us
    all_gather x1 -> x0, waiting for transfers between devices: 72.6 us -> none  [shards(): weights = lax.all_gather(qkv_weight, 'dp', axis=0, tiled=True)]
    pallas_call x0 -> x1, Pallas kernels: none -> 68.8 us  [shards(): pl.pallas_call(functools.partial(kernel, sizes), out_shape=(jax.ShapeDtyp...]
    reduce_scatter x1, waiting for transfers between devices: 0.01 us -> 40.5 us  [shards(): share = lax.psum_scatter(share, 'seq', scatter_dimension=0, tiled=True)]
    dot_general x9 -> x0, matrix products: 33 us -> none  [the longest x1 6.78 us: project_back(): lax.dot_general(flat, weights, (((1,), (1,)), ((), ())), preferred_elemen...]
    all_to_all x1 -> x0, blocking collectives: 26.4 us -> none  [shards(): lax.all_to_all(grad_packed, 'seq', split_axis=0, concat_axis=1, tiled=True)]
    reshape x3 -> x0, local copies, waits for them, and re-layouts: 18.5 us -> none  [the longest x2 12.1 us: project_rows(): return jnp.dot(rows_in.reshape(-1, rows_in.shape[-1]), weights, preferred...]
    all_to_all x2 -> x0, waiting for transfers between devices: 17.6 us -> none  [the longest x1 17.6 us: shards(): lax.all_to_all(packed_frames, 'seq', split_axis=1, concat_axis=0, tiled=T...]
    unnamed x4 -> x3, waiting for transfers between devices: 17 us -> 29.8 us
  transfers between devices with their start and end apart: 5 -> 2, of which waited for: 3 -> 2; matrix products, arithmetic and copies ran while one was open for 27% -> 0% of each run, Pallas kernels for 0% -> 0%
where the time goes in v1:
time: 161 us
  waiting for transfers between devices  70.3 us (44%)
  Pallas kernels  68.8 us (43%)
  between operations  14 us (9%)
  local copies, waits for them, and re-layouts  7.96 us (5%)
    pallas_call x1, Pallas kernels, shards(): pl.pallas_call(functools.partial(kernel, sizes), out_shape=(jax.ShapeDtyp...  68.8 us
    reduce_scatter x1, waiting for transfers between devices, shards(): share = lax.psum_scatter(share, 'seq', scatter_dimension=0, tiled=True)  40.5 us
    unnamed x3, waiting for transfers between devices  29.8 us
    unnamed x6, local copies, waits for them, and re-layouts  6.6 us
  transfers between devices with their start and end apart: 2, of which 2 were waited for; matrix products, arithmetic and copies ran while one was open for 0% of the time, Pallas kernels for 0%

profile of v1, /device:TPU:0, one launch (start us, length us, event | category | flops | bytes accessed | tf_op | source)
XLA Modules:
  0.0 161.1 jit_solution(13544891779385618601)
XLA Ops:
  7.2 0.0 reduce-scatter.5.cloned.1.call-start
  7.2 1.3 copy.13
  8.5 0.7 tile.4
  9.2 0.1 tile.10
  9.3 0.6 pad.4.gains
  9.9 68.8 %shard_map.86 = (bf16[2,256,1152]{2,1,0:T(8,128)(2,1)}, f32[576,1152]{1,0:T(8,128)}) custom-call(bf16[2,256,1152]{2,1,0:T(8,128)(2,1)} %bitcast.12, bf16[2,256,1152]{2,1,0:T(8,128)(2,1)} %bitcast.13, bf16[288,1728]{1,0:T(8,128)(2,1)} %w_in.1, f32[3,1152]{1,0:T(4,128)} %bitcast.11, f32[2,640]{1,0:T(2,128)} %pad.4.gains, bf16[576,1152]{1,0:T(8,128)(2,1)} %out_w.1, ...), custom_call_target="tpu_custom_call" | custom-call | flops 12000000000 | bytes 20000000 | tf_op jit(solution)/shard_map/pallas_call | solution.py:400
  78.7 0.0 reduce-scatter.5.cloned.1.call-update
  78.7 0.0 reduce-scatter.7.cloned.1.call-start
  78.7 40.5 %reduce-scatter.5.cloned.1.call-done = f32[144,1152]{1,0:T(8,128)} async-done(((f32[576,1152]{1,0:T(8,128)}), f32[144,1152]{1,0:T(8,128)}) %reduce-scatter.5.cloned.1.call-update) | async-done | bytes 663568 | tf_op jit(solution)/shard_map/reduce_scatter | solution.py:439
  119.3 2.5 %copy.9 = f32[144,1152]{0,1:T(8,128)} copy(f32[144,1152]{1,0:T(8,128)} %reduce-scatter.5.cloned.1.call-done) | data formatting | bytes 1327104
  121.7 0.0 copy-start
  121.7 0.0 reduce-scatter.7.cloned.1.call-update
  121.8 29.7 %reduce-scatter.7.cloned.1.call-done = f32[288,144]{1,0:T(8,128)} async-done(((f32[1152,144]{1,0:T(8,128)}), f32[288,144]{1,0:T(8,128)}) %reduce-scatter.7.cloned.1.call-update) | async-done | bytes 165904
  151.5 1.8 %copy.10 = f32[144,288]{1,0:T(8,128)} copy(f32[144,288]{0,1:T(8,128)} %bitcast.10) | data formatting | bytes 331776
  153.3 0.0 copy-done
  153.3 1.0 copy.15
Async XLA Ops:
  7.2 112.1 %reduce-scatter.5.cloned.1.call-start = ((), (), s32[]{:S(2)}) async-start(), calls=%async_computation.2 | async-start | bytes 3317760 | tf_op jit(solution)/shard_map/reduce_scatter | solution.py:439
  78.7 72.8 %reduce-scatter.7.cloned.1.call-start = ((), (), s32[]{:S(2)}) async-start(), calls=%async_computation.3 | async-start | bytes 1474560
  121.7 31.6 %copy-start = (bf16[2,256,1152]{2,1,0:T(8,128)(2,1)S(1)}, bf16[2,256,1152]{2,1,0:T(8,128)(2,1)}, u32[]{:S(2)}) copy-start(bf16[2,256,1152]{2,1,0:T(8,128)(2,1)} %get-tuple-element.4) | copy-start | bytes 3538948
Sparse Core Ops, SparseCore 0:
  78.8 40.3 reduce-scatter.4
  122.2 29.1 reduce-scatter.6

commit v2 on v1

--- a/solution.py
+++ b/solution.py
@@ -64,7 +64,7 @@
     cotangent,
     w_in,
     mod,
-    gains,
+    gain_in,
     out_w,
     ones,
     grad_hidden,
@@ -91,8 +91,17 @@
     w_send,
     w_recv,
     w_own,
+    share_s,
+    pair_out,
+    pair_in,
+    far_out,
+    far_in,
+    col_out,
+    col_in,
+    g_send,
+    g_recv,
 ):
-    nseq, ndp, frames, chunks, tokens, width, gather_here = sizes
+    nseq, ndp, frames, chunks, tokens, width, gather_here, reduce_here = sizes
     mine = frames // nseq
     rows = frames * tokens
     block = chunks * tokens
@@ -107,13 +116,15 @@
     count = nseq - 1
     for peer in seq_peers:
         pl.semaphore_signal(barrier, inc=1, device_id={"seq": peer}, device_id_type=MESH)
-    if gather_here:
+    if gather_here or reduce_here:
         for i in range(1, ndp):
             pl.semaphore_signal(
                 barrier, inc=1, device_id={"dp": lax.rem(dp + i, ndp)}, device_id_type=MESH
             )
+        count += ndp - 1
+    if gather_here:
         pl.semaphore_signal(barrier, inc=1, device_id={"groups": 1 - group}, device_id_type=MESH)
-        count += ndp
+        count += 1
     pl.semaphore_wait(barrier, count)
 
     def frames_of(device):
@@ -251,6 +262,7 @@
 
     own_weights.wait()
 
+    gains = jnp.concatenate([gain_in[...]] * HEADS + [jnp.zeros((2, PAD - WIDE), F32)], axis=1)
     scale = HD ** (-0.5)
     k_low = WIDE - (PAD - WIDE)
     v_low = 2 * WIDE
@@ -307,18 +319,82 @@
         ga = dot_nt(gated, out_w[...]).astype(BF16)
         ga_s[chunk] = jnp.concatenate([ga, jnp.zeros((rows, PAD - WIDE), BF16)], axis=1)
         share = dot_tn(att_s[chunk][:, 0:WIDE], gated)
+        target = share_s if reduce_here else grad_w
+        share = share.reshape(target.shape)
 
         @pl.when(chunk == 0)
         def _():
-            grad_w[...] = share
+            target[...] = share
 
         @pl.when(chunk > 0)
         def _():
-            grad_w[...] += share
+            target[...] += share
 
         return carry
 
     lax.fori_loop(0, chunks, middle, 0)
+
+    chips = nseq // 2
+    chip = lax.div(seq, 2)
+    columns = width // ndp
+
+    def to_pair():
+        return pltpu.make_async_remote_copy(
+            src_ref=pair_out,
+            dst_ref=pair_in,
+            send_sem=g_send.at[0],
+            recv_sem=g_recv.at[0],
+            device_id=to_core,
+            device_id_type=MESH,
+        )
+
+    def to_chip(i):
+        return pltpu.make_async_remote_copy(
+            src_ref=far_out.at[i - 1],
+            dst_ref=far_in.at[i - 1],
+            send_sem=g_send.at[i],
+            recv_sem=g_recv.at[i],
+            device_id={"seq": lax.rem(chip + i, chips) * 2 + core},
+            device_id_type=MESH,
+        )
+
+    def to_columns(i):
+        return pltpu.make_async_remote_copy(
+            src_ref=col_out.at[lax.rem(dp + i, ndp)],
+            dst_ref=col_in.at[i - 1],
+            send_sem=g_send.at[chips + i - 1],
+            recv_sem=g_recv.at[chips + i - 1],
+            device_id={"dp": lax.rem(dp + i, ndp)},
+            device_id_type=MESH,
+        )
+
+    def reduce_chips():
+        to_pair().wait()
+        for i in range(1, chips):
+            there = lax.rem(chip + i, chips)
+            far_out[i - 1] = (share_s[there * 2 + core] + pair_in[there].astype(F32)).astype(BF16)
+            to_chip(i).start()
+
+    def reduce_columns():
+        total = share_s[seq] + pair_in[chip].astype(F32)
+        for i in range(1, chips):
+            to_chip(i).wait()
+            total = total + far_in[i - 1].astype(F32)
+        for d in range(ndp):
+            part = total[:, d * columns : (d + 1) * columns]
+            col_out[d] = part.astype(BF16)
+
+            @pl.when(dp == d)
+            def _():
+                grad_w[...] = part
+
+        for i in range(1, ndp):
+            to_columns(i).start()
+
+    if reduce_here:
+        for c in range(chips):
+            pair_out[c] = share_s[2 * c + 1 - core].astype(BF16)
+        to_pair().start()
 
     def backward(chunk, carry):
         qn = qn_s[chunk]
@@ -366,9 +442,20 @@
         for i in range(nseq - 1):
             outward(chunk, i).start()
         outward_own(chunk).start()
+        if reduce_here:
+
+            @pl.when(chunk == 0)
+            def _():
+                reduce_chips()
+
         return carry
 
     lax.fori_loop(0, chunks, backward, 0)
+    if reduce_here:
+        reduce_columns()
+        for i in range(1, ndp):
+            to_columns(i).wait()
+            grad_w[...] += col_in[i - 1].astype(F32)
     for chunk in range(chunks):
         for i in range(nseq - 1):
             outward(chunk, i).wait()
@@ -385,11 +472,27 @@
     gather_here = qkv_weight.shape[0] % 32 == 0
     if not gather_here:
         qkv_weight = lax.all_gather(qkv_weight, "dp", axis=0, tiled=True)
-    gains = jnp.pad(jnp.tile(qk_gain, (1, HEADS)), ((0, 0), (0, PAD - WIDE)))
     lane = np.arange(PAD)
     inside = (lane < WIDE)[:, None] & (lane[:, None] // HD == lane[None, :] // HD)
     ones = jnp.asarray(inside.astype(np.float32), BF16)
-    sizes = (nseq, ndp, frames, chunks, tokens, width, gather_here)
+    out_rows = WIDE // nseq
+    columns = width // ndp
+    reduce_here = out_rows % 16 == 0
+    sizes = (nseq, ndp, frames, chunks, tokens, width, gather_here, reduce_here)
+    if reduce_here:
+        share_shape = (out_rows, columns)
+        share_scratch = [
+            pltpu.VMEM((nseq, out_rows, width), F32),
+            pltpu.VMEM((nseq // 2, out_rows, width), BF16),
+            pltpu.VMEM((nseq // 2, out_rows, width), BF16),
+            pltpu.VMEM((nseq // 2 - 1, out_rows, width), BF16),
+            pltpu.VMEM((nseq // 2 - 1, out_rows, width), BF16),
+            pltpu.VMEM((ndp, out_rows, columns), BF16),
+            pltpu.VMEM((ndp - 1, out_rows, columns), BF16),
+        ]
+    else:
+        share_shape = (WIDE, width)
+        share_scratch = [pltpu.VMEM((16, LANES), F32)] * 7
     anywhere = pl.BlockSpec(memory_space=pl.ANY)
     vmem = pl.BlockSpec(memory_space=pltpu.VMEM)
 
@@ -401,7 +504,7 @@
         functools.partial(kernel, sizes),
         out_shape=(
             jax.ShapeDtypeStruct((mine, all_tokens, width), BF16),
-            jax.ShapeDtypeStruct((WIDE, width), F32),
+            jax.ShapeDtypeStruct(share_shape, F32),
         ),
         in_specs=[anywhere, anywhere, anywhere, vmem, vmem, vmem, vmem],
         out_specs=(anywhere, vmem),
@@ -428,6 +531,9 @@
             pltpu.SemaphoreType.DMA((4, ndp)),
             pltpu.SemaphoreType.DMA((4, ndp)),
             pltpu.SemaphoreType.DMA,
+            *share_scratch,
+            pltpu.SemaphoreType.DMA((nseq // 2 + ndp,)),
+            pltpu.SemaphoreType.DMA((nseq // 2 + ndp,)),
         ],
         compiler_params=pltpu.CompilerParams(
             collective_id=0, has_side_effects=True, vmem_limit_bytes=56 * 2**20
@@ -435,9 +541,10 @@
         cost_estimate=pl.CostEstimate(
             flops=12_000_000_000, bytes_accessed=20_000_000, transcendentals=2_000_000
         ),
-    )(hidden_states[0], out_cotangent[0], qkv_weight, modulation[0], gains, out_weight, ones)
-    share = lax.psum_scatter(share, "seq", scatter_dimension=0, tiled=True)
-    share = lax.psum_scatter(share, "dp", scatter_dimension=1, tiled=True)
+    )(hidden_states[0], out_cotangent[0], qkv_weight, modulation[0], qk_gain, out_weight, ones)
+    if not reduce_here:
+        share = lax.psum_scatter(share, "seq", scatter_dimension=0, tiled=True)
+        share = lax.psum_scatter(share, "dp", scatter_dimension=1, tiled=True)
     return (grad_hidden[None], share)
 
 

time: 161 us -> 89.5 us (0.56)
  waiting for transfers between devices: 70.3 us -> 0 us
  Pallas kernels: 68.8 us -> 84.2 us
  between operations: 14 us -> 0.65 us
  local copies, waits for them, and re-layouts: 7.96 us -> 4.43 us
    reduce_scatter x1 -> x0, waiting for transfers between devices: 40.5 us -> none  [shards(): share = lax.psum_scatter(share, 'seq', scatter_dimension=0, tiled=True)]
    unnamed x3 -> x0, waiting for transfers between devices: 29.8 us -> none
    pallas_call x1, Pallas kernels: 68.8 us -> 84.2 us  [shards(): pl.pallas_call(functools.partial(kernel, sizes), out_shape=(jax.ShapeDtyp...]
    unnamed x6 -> x5, local copies, waits for them, and re-layouts: 6.6 us -> 4.43 us
  transfers between devices with their start and end apart: 2 -> 0, of which waited for: 2 -> 0; matrix products, arithmetic and copies ran while one was open for 0% -> 0% of each run, Pallas kernels for 0% -> 0%
where the time goes in v2:
time: 89.5 us; the launch traced here: 89.3 us
  Pallas kernels  84.2 us (94%)
  local copies, waits for them, and re-layouts  4.43 us (5%)
    pallas_call x1, Pallas kernels, shards(): pl.pallas_call(functools.partial(kernel, sizes), out_shape=(jax.ShapeDtyp...  84.2 us
    unnamed x5, local copies, waits for them, and re-layouts  4.43 us

profile of v2, /device:TPU:0, one launch (start us, length us, event | category | flops | bytes accessed | tf_op | source)
XLA Modules:
  0.0 89.3 jit_solution(13173167237523592989)
XLA Ops:
  0.6 1.3 %copy.11 = f32[1,3,1152]{2,1,0:T(4,128)} copy(f32[1,3,1152]{2,0,1:T(1,128)} %param.8) | data formatting | bytes 27648
  2.0 84.2 %shard_map.86 = (bf16[2,256,1152]{2,1,0:T(8,128)(2,1)}, f32[144,288]{1,0:T(8,128)}) custom-call(bf16[2,256,1152]{2,1,0:T(8,128)(2,1)} %bitcast.8, bf16[2,256,1152]{2,1,0:T(8,128)(2,1)} %bitcast.9, bf16[288,1728]{1,0:T(8,128)(2,1)} %w_in.1, f32[3,1152]{1,0:T(4,128)} %bitcast.7, f32[2,72]{1,0:T(2,128)} %gain_in.1, bf16[576,1152]{1,0:T(8,128)(2,1)} %out_w.1, ...), custom_call_target="tpu_custom_call" | custom-call | flops 12000000000 | bytes 20000000 | tf_op jit(solution)/shard_map/pallas_call | solution.py:503
  86.2 0.0 copy-start
  86.2 2.4 %copy.14 = bf16[1,2,256,1152]{3,2,1,0:T(8,128)(2,1)} copy(bf16[1,2,256,1152]{3,2,1,0:T(8,128)(2,1)} %bitcast.6) | data formatting | bytes 2359296
  88.6 0.0 copy-done
  88.6 0.7 copy.15
Async XLA Ops:
  86.2 2.4 %copy-start = (f32[144,288]{1,0:T(8,128)S(1)}, f32[144,288]{1,0:T(8,128)}, u32[]{:S(2)}) copy-start(f32[144,288]{1,0:T(8,128)} %get-tuple-element.9) | copy-start | bytes 497668

commit v3 on v2

--- a/solution.py
+++ b/solution.py
@@ -36,9 +36,14 @@
 
 
 def head_sum(values, ones):
-    high = values.astype(BF16)
-    low = (values - high.astype(F32)).astype(BF16)
-    return dot_nn(high, ones) + dot_nn(low, ones)
+    values = values.astype(BF16)
+    parts = []
+    for low in range(0, PAD, 256):
+        high = min(low + 256, PAD)
+        first = low // HD * HD // LANES * LANES
+        last = min(-(-(-(-high // HD) * HD) // LANES) * LANES, PAD)
+        parts.append(dot_nn(values[:, first:last], ones[first:last, low:high]))
+    return jnp.concatenate(parts, axis=1)
 
 
 def head_window(array, head, masked):
@@ -74,6 +79,7 @@
     gh_tok,
     weights,
     normed_s,
+    modulated_s,
     rinv_s,
     q_s,
     k_s,
@@ -211,63 +217,15 @@
         )
     else:
         own_weights = pltpu.make_async_copy(w_in, weights, w_own)
-    for kind in range(2):
-        for chunk in range(chunks):
-            for i in range(nseq - 1):
-                inward(kind, chunk, i).start()
+    for chunk in range(chunks):
+        for i in range(nseq - 1):
+            inward(0, chunk, i).start()
     own_weights.start()
     for kind in range(2):
         for chunk in range(chunks):
             inward_own(kind, chunk).start()
 
-    if gather_here:
-
-        def relays(i):
-            return lax.rem(lax.rem(dp + ndp - i, ndp), 2) == core
-
-        for i in range(1, ndp):
-
-            @pl.when(relays(i))
-            def _():
-                along_dp(i).wait_recv()
-                hand_on(1, i, group, to_group).start()
-                hand_on(2, i, group, to_core).start()
-
-        for i in range(1, ndp):
-
-            @pl.when(relays(i))
-            def _():
-                hand_on(1, i, 1 - group, to_group).wait_recv()
-                hand_on(3, i, 1 - group, to_core).start()
-
-        for i in range(1, ndp):
-
-            @pl.when(jnp.logical_not(relays(i)))
-            def _():
-                hand_on(2, i, group, to_core).wait_recv()
-                hand_on(3, i, 1 - group, to_core).wait_recv()
-
-        for i in range(1, ndp):
-
-            @pl.when(relays(i))
-            def _():
-                hand_on(1, i, group, to_group).wait_send()
-                hand_on(2, i, group, to_core).wait_send()
-                hand_on(3, i, 1 - group, to_core).wait_send()
-
-        @pl.when(lax.rem(dp, 2) == core)
-        def _():
-            for i in range(1, ndp):
-                along_dp(i).wait_send()
-
-    own_weights.wait()
-
-    gains = jnp.concatenate([gain_in[...]] * HEADS + [jnp.zeros((2, PAD - WIDE), F32)], axis=1)
-    scale = HD ** (-0.5)
-    k_low = WIDE - (PAD - WIDE)
-    v_low = 2 * WIDE
-
-    def forward(chunk, carry):
+    def norm(chunk, carry):
         for i in range(nseq - 1):
             inward(0, chunk, i).wait()
         inward_own(0, chunk).wait()
@@ -277,7 +235,59 @@
         normed = centered * rinv
         normed_s[chunk] = normed
         rinv_s[chunk] = rinv
-        modulated = (normed * (1.0 + mod[1:2, :]) + mod[0:1, :]).astype(BF16)
+        modulated_s[chunk] = (normed * (1.0 + mod[1]) + mod[0]).astype(BF16)
+        return carry
+
+    def second_array():
+        for chunk in range(chunks):
+            for i in range(nseq - 1):
+                inward(1, chunk, i).start()
+
+    if gather_here:
+        order = [jnp.where(dp == 0, ndp - i, i) for i in range(1, ndp)]
+
+        def relays(i):
+            return lax.rem(lax.rem(dp + ndp - i, ndp), 2) == core
+
+        def from_dp(i):
+            @pl.when(relays(i))
+            def _():
+                along_dp(i).wait_recv()
+                hand_on(1, i, group, to_group).start()
+                hand_on(2, i, group, to_core).start()
+
+        def from_group(i):
+            @pl.when(relays(i))
+            def _():
+                hand_on(1, i, 1 - group, to_group).wait_recv()
+                hand_on(3, i, 1 - group, to_core).start()
+
+        from_dp(order[0])
+        lax.fori_loop(0, chunks, norm, 0)
+        second_array()
+        for i in order[1:]:
+            from_dp(i)
+        for i in order:
+            from_group(i)
+        for i in order:
+
+            @pl.when(jnp.logical_not(relays(i)))
+            def _():
+                hand_on(2, i, group, to_core).wait_recv()
+                hand_on(3, i, 1 - group, to_core).wait_recv()
+
+    else:
+        lax.fori_loop(0, chunks, norm, 0)
+        second_array()
+    own_weights.wait()
+
+    gains = jnp.concatenate([gain_in[...]] * HEADS + [jnp.zeros((2, PAD - WIDE), F32)], axis=1)
+    scale = HD ** (-0.5)
+    k_low = WIDE - (PAD - WIDE)
+    v_low = 2 * WIDE
+
+    def forward(chunk, carry):
+        modulated = modulated_s[chunk]
         q = dot_nn(modulated, weights[:, 0:PAD]).astype(BF16)
         k = pltpu.roll(dot_nn(modulated, weights[:, k_low : k_low + PAD]), WIDE, 1).astype(BF16)
         v = dot_nn(modulated, weights[:, v_low : v_low + WIDE]).astype(BF16)
@@ -287,8 +297,8 @@
         v_s[chunk] = v
         q32 = q.astype(F32)
         k32 = k.astype(F32)
-        rq = lax.rsqrt(head_sum(q32 * q32, ones[...]) * (1.0 / HD) + EPS)
-        rk = lax.rsqrt(head_sum(k32 * k32, ones[...]) * (1.0 / HD) + EPS)
+        rq = lax.rsqrt(head_sum(q32 * q32, ones) * (1.0 / HD) + EPS)
+        rk = lax.rsqrt(head_sum(k32 * k32, ones) * (1.0 / HD) + EPS)
         rq_s[chunk] = rq
         rk_s[chunk] = rk
         qn = (q32 * rq * gains[0:1, :]).astype(BF16)
@@ -315,7 +325,7 @@
         for i in range(nseq - 1):
             inward(1, chunk, i).wait()
         inward_own(1, chunk).wait()
-        gated = (mod[2:3, :] * cot_tok[chunk].reshape(rows, width).astype(F32)).astype(BF16)
+        gated = (mod[2] * cot_tok[chunk].reshape(rows, width).astype(F32)).astype(BF16)
         ga = dot_nt(gated, out_w[...]).astype(BF16)
         ga_s[chunk] = jnp.concatenate([ga, jnp.zeros((rows, PAD - WIDE), BF16)], axis=1)
         share = dot_tn(att_s[chunk][:, 0:WIDE], gated)
@@ -417,7 +427,7 @@
         def through_norm(raw, inverse, gain, grads):
             raw = raw.astype(F32)
             scaled = jnp.concatenate(grads, axis=1) * gain
-            mean = head_sum(raw * scaled, ones[...]) * (1.0 / HD)
+            mean = head_sum(raw * scaled, ones) * (1.0 / HD)
             return inverse * scaled - raw * inverse * inverse * inverse * mean
 
         grad_q = through_norm(q_s[chunk], rq_s[chunk], gains[0:1, :], grad_qn).astype(BF16)
@@ -431,7 +441,7 @@
             + dot_nt(grad_v, weights[:, v_low : v_low + WIDE])
         ).astype(BF16)
         normed = normed_s[chunk]
-        grad_normed = grad_mod.astype(F32) * (1.0 + mod[1:2, :])
+        grad_normed = grad_mod.astype(F32) * (1.0 + mod[1])
         grad_ln = rinv_s[chunk] * (
             grad_normed
             - jnp.mean(grad_normed, -1, keepdims=True)
@@ -456,6 +466,20 @@
         for i in range(1, ndp):
             to_columns(i).wait()
             grad_w[...] += col_in[i - 1].astype(F32)
+    if gather_here:
+        for i in order:
+
+            @pl.when(relays(i))
+            def _():
+                hand_on(1, i, group, to_group).wait_send()
+                hand_on(2, i, group, to_core).wait_send()
+                hand_on(3, i, 1 - group, to_core).wait_send()
+
+        @pl.when(lax.rem(dp, 2) == core)
+        def _():
+            for i in range(1, ndp):
+                along_dp(i).wait_send()
+
     for chunk in range(chunks):
         for i in range(nseq - 1):
             outward(chunk, i).wait()
@@ -514,6 +538,7 @@
             by_token,
             pltpu.VMEM((width, 3 * WIDE), BF16),
             pltpu.VMEM((chunks, rows, width), F32),
+            pltpu.VMEM((chunks, rows, width), BF16),
             pltpu.VMEM((chunks, rows, 1), F32),
             wide(BF16),
             wide(BF16),
@@ -541,7 +566,7 @@
         cost_estimate=pl.CostEstimate(
             flops=12_000_000_000, bytes_accessed=20_000_000, transcendentals=2_000_000
         ),
-    )(hidden_states[0], out_cotangent[0], qkv_weight, modulation[0], qk_gain, out_weight, ones)
+    )(hidden_states[0], out_cotangent[0], qkv_weight, modulation.transpose(1, 0, 2), qk_gain, out_weight, ones)
     if not reduce_here:
         share = lax.psum_scatter(share, "seq", scatter_dimension=0, tiled=True)
         share = lax.psum_scatter(share, "dp", scatter_dimension=1, tiled=True)

time: 89.5 us -> 84 us (0.939)
  Pallas kernels: 84.2 us -> 80.1 us
  local copies, waits for them, and re-layouts: 4.43 us -> 3.1 us
    pallas_call x1, Pallas kernels: 84.2 us -> 80.1 us  [shards(): pl.pallas_call(functools.partial(kernel, sizes), out_shape=(jax.ShapeDtyp...]
    unnamed x5 -> x4, local copies, waits for them, and re-layouts: 4.43 us -> 3.1 us
where the time goes in v3:
time: 84 us; the launch traced here: 83.8 us
  Pallas kernels  80.1 us (95%)
  local copies, waits for them, and re-layouts  3.1 us (4%)
    pallas_call x1, Pallas kernels, shards(): pl.pallas_call(functools.partial(kernel, sizes), out_shape=(jax.ShapeDtyp...  80.1 us
    unnamed x4, local copies, waits for them, and re-layouts  3.1 us

profile of v3, /device:TPU:0, one launch (start us, length us, event | category | flops | bytes accessed | tf_op | source)
XLA Modules:
  0.0 83.8 jit_solution(1410154043073418207)
XLA Ops:
  0.6 80.1 %shard_map.86 = (bf16[2,256,1152]{2,1,0:T(8,128)(2,1)}, f32[144,288]{1,0:T(8,128)}) custom-call(bf16[2,256,1152]{2,1,0:T(8,128)(2,1)} %bitcast.5, bf16[2,256,1152]{2,1,0:T(8,128)(2,1)} %bitcast.6, bf16[288,1728]{1,0:T(8,128)(2,1)} %w_in.1, f32[3,1,1152]{2,1,0:T(1,128)} %bitcast.7, f32[2,72]{1,0:T(2,128)} %gain_in.1, bf16[576,1152]{1,0:T(8,128)(2,1)} %out_w.1, ...), custom_call_target="tpu_custom_call" | custom-call | flops 12000000000 | bytes 20000000 | tf_op jit(solution)/shard_map/pallas_call | solution.py:527
  80.7 0.0 copy-start
  80.7 2.4 %copy.11 = bf16[1,2,256,1152]{3,2,1,0:T(8,128)(2,1)} copy(bf16[1,2,256,1152]{3,2,1,0:T(8,128)(2,1)} %bitcast.4) | data formatting | bytes 2359296
  83.1 0.0 copy-done
  83.1 0.7 copy.12
Async XLA Ops:
  80.7 2.4 %copy-start = (f32[144,288]{1,0:T(8,128)S(1)}, f32[144,288]{1,0:T(8,128)}, u32[]{:S(2)}) copy-start(f32[144,288]{1,0:T(8,128)} %get-tuple-element.9) | copy-start | bytes 497668

commit v4 on v3

--- a/solution.py
+++ b/solution.py
@@ -265,9 +265,10 @@
         from_dp(order[0])
         lax.fori_loop(0, chunks, norm, 0)
         second_array()
+        from_group(order[0])
         for i in order[1:]:
             from_dp(i)
-        for i in order:
+        for i in order[1:]:
             from_group(i)
         for i in order:
 
@@ -458,11 +459,18 @@
             def _():
                 reduce_chips()
 
+            if chunks > 2:
+
+                @pl.when(chunk == chunks - 2)
+                def _():
+                    reduce_columns()
+
         return carry
 
     lax.fori_loop(0, chunks, backward, 0)
     if reduce_here:
-        reduce_columns()
+        if chunks <= 2:
+            reduce_columns()
         for i in range(1, ndp):
             to_columns(i).wait()
             grad_w[...] += col_in[i - 1].astype(F32)
@@ -490,7 +498,7 @@
     mine, all_tokens, width = hidden_states.shape[1:]
     frames = mine * nseq
     block = all_tokens // nseq
-    tokens = min(block, max(16, 256 // frames))
+    tokens = min(block, max(16, 128 // frames))
     chunks = block // tokens
     rows = frames * tokens
     gather_here = qkv_weight.shape[0] % 32 == 0

time: 84 us -> 85.8 us (1.021)
  Pallas kernels: 80.1 us -> 81.7 us
    pallas_call x1, Pallas kernels: 80.1 us -> 81.7 us  [shards(): pl.pallas_call(functools.partial(kernel, sizes), out_shape=(jax.ShapeDtyp...]
where the time goes in v4:
time: 85.8 us; the launch traced here: 85.4 us
  Pallas kernels  81.7 us (95%)
  local copies, waits for them, and re-layouts  3.1 us (4%)
    pallas_call x1, Pallas kernels, shards(): pl.pallas_call(functools.partial(kernel, sizes), out_shape=(jax.ShapeDtyp...  81.7 us
    unnamed x4, local copies, waits for them, and re-layouts  3.1 us

profile of v4, /device:TPU:0, one launch (start us, length us, event | category | flops | bytes accessed | tf_op | source)
XLA Modules:
  0.0 85.4 jit_solution(9213981033515237085)
XLA Ops:
  0.6 81.7 %shard_map.86 = (bf16[2,256,1152]{2,1,0:T(8,128)(2,1)}, f32[144,288]{1,0:T(8,128)}) custom-call(bf16[2,256,1152]{2,1,0:T(8,128)(2,1)} %bitcast.5, bf16[2,256,1152]{2,1,0:T(8,128)(2,1)} %bitcast.6, bf16[288,1728]{1,0:T(8,128)(2,1)} %w_in.1, f32[3,1,1152]{2,1,0:T(1,128)} %bitcast.7, f32[2,72]{1,0:T(2,128)} %gain_in.1, bf16[576,1152]{1,0:T(8,128)(2,1)} %out_w.1, ...), custom_call_target="tpu_custom_call" | custom-call | flops 12000000000 | bytes 20000000 | tf_op jit(solution)/shard_map/pallas_call | solution.py:535
  82.3 0.0 copy-start
  82.3 2.4 %copy.11 = bf16[1,2,256,1152]{3,2,1,0:T(8,128)(2,1)} copy(bf16[1,2,256,1152]{3,2,1,0:T(8,128)(2,1)} %bitcast.4) | data formatting | bytes 2359296
  84.7 0.0 copy-done
  84.8 0.7 copy.12
Async XLA Ops:
  82.3 2.4 %copy-start = (f32[144,288]{1,0:T(8,128)S(1)}, f32[144,288]{1,0:T(8,128)}, u32[]{:S(2)}) copy-start(f32[144,288]{1,0:T(8,128)} %get-tuple-element.9) | copy-start | bytes 497668
